TPU v7x, 32 devices: a whole 2x2x4 slice. The times are simulated.
32 devices in a mesh: space: 16 (over z, y, core), mem: 2 (over x).
Axes of the slice: x: 2, y: 2, z: 4, core: 2. Of those that a mesh axis runs over, the one named last changes fastest.
Arguments:
- state: float32 [64, 262144], P('mem', 'space'), may hold values from -6 to 6
- obs_index: int32 [4, 4096], P(None, 'space'), may hold values from 0 to 262143, as said below
- obs_value: float32 [4, 4096], P(None, 'space'), may hold values from -8 to 8
- obs_var: float32 [4, 4096], P(None, 'space'), may hold values from 0.02 to 5
Outputs:
- posterior: float32 [64, 262144], P('mem', 'space')
Inputs may be any that keep to these rules, and one draw needn't show every extreme that they name: `obs_index`: observation k of every batch measures a column of the block owned by index k // 256 of space, that is a column between (k // 256) * 16384 and (k // 256 + 1) * 16384 - 1.
All inputs are finite; a program needn't handle non-finite values.
Results may differ from a plain program's by a relative error of at most 0.0075.
Values may be sent and summed in bfloat16 or wider, within the bound.
A program may use at most 64 MiB of HBM per device.

v0:
```python
import jax
import jax.numpy as jnp
from jax import lax
from jax.sharding import PartitionSpec as P

RADIUS = 32768


def shifted(block, axis, distance):
    devices = range(lax.axis_size(axis))
    route = [(i - distance, i) for i in devices if i - distance in devices]
    return lax.ppermute(block, axis, route)


def summarize(prior_obs, values, variances):
    members = prior_obs.shape[0]
    obs_mean = jnp.mean(prior_obs, axis=0)
    anomaly = prior_obs - obs_mean
    spread = jnp.sum(anomaly * anomaly, axis=0) / (members - 1) + 1e-06
    post_var = 1.0 / (1.0 / spread + 1.0 / variances)
    post_mean = post_var * (obs_mean / spread + values / variances)
    change = post_mean - obs_mean + (jnp.sqrt(post_var / spread) - 1.0) * anomaly
    weighted = (change / ((members - 1) * spread)).astype(jnp.bfloat16)
    return (anomaly.astype(jnp.bfloat16), weighted)


def position_band(obs_index):
    pieces = []
    for offset in (2, 1, 0, -1, -2):
        if offset == 0:
            pieces.append(obs_index)
        else:
            pieces.append(shifted(obs_index, "space", offset))
    return jnp.concatenate(pieces, axis=1)


def prior_band(packed):
    pieces = []
    for offset in (2, 1, 0, -1, -2):
        if offset == 0:
            pieces.append(packed)
        else:
            pieces.append(shifted(packed, "space", offset))
    return jnp.concatenate(pieces, axis=1)


def shards(state, obs_index, obs_value, obs_var):
    mem_index = lax.axis_index("mem")
    space_index = lax.axis_index("space")
    pair_count = lax.axis_size("mem")
    columns = lax.all_to_all(state, "mem", split_axis=1, concat_axis=0, tiled=True)
    width = columns.shape[1]
    col_start = space_index * (pair_count * width) + mem_index * width
    members = columns.shape[0]
    band_positions = position_band(obs_index)
    block_width = min(1024, state.shape[1] // 2)
    block_count = width // block_width
    column_base = col_start + lax.iota(jnp.int32, block_width)
    for batch in range(obs_index.shape[0]):
        local_col = obs_index[batch] - col_start
        inside = (local_col >= 0) & (local_col < width)
        picked = jnp.take(columns, jnp.clip(local_col, 0, width - 1), axis=1)
        partial_value = jnp.where(inside[None, :], picked, 0.0)
        packed = jnp.concatenate(
            [partial_value, obs_value[batch][None, :], obs_var[batch][None, :]], axis=0
        )
        band_raw = prior_band(packed)
        band_prior = band_raw[:members]
        band_prior = lax.psum(band_prior, "mem")
        values = band_raw[members]
        variances = jnp.where(band_raw[members + 1] > 0.0, band_raw[members + 1], 1.0)
        band_anom, band_weight = summarize(band_prior, values, variances)
        band_pos = band_positions[batch]
        state_anom = (columns - jnp.mean(columns, axis=0)).astype(jnp.bfloat16)

        def update(step, current):
            block_start = step * block_width
            spread_piece = lax.dynamic_slice_in_dim(state_anom, block_start, block_width, 1)
            cov = lax.dot_general(
                band_anom,
                spread_piece,
                (((0,), (0,)), ((), ())),
                preferred_element_type=jnp.float32,
            )
            distance = jnp.abs(column_base[None, :] + block_start - band_pos[:, None]).astype(
                jnp.float32
            )
            taper = jnp.square(jnp.maximum(0.0, 1.0 - distance / RADIUS))
            gain = (taper * cov).astype(jnp.bfloat16)
            increment = jnp.dot(band_weight, gain, preferred_element_type=jnp.float32)
            before = lax.dynamic_slice_in_dim(current, block_start, block_width, 1)
            return lax.dynamic_update_slice_in_dim(current, before + increment, block_start, 1)

        columns = lax.fori_loop(0, block_count, update, columns)
    return lax.all_to_all(
        columns.astype(jnp.bfloat16), "mem", split_axis=0, concat_axis=1, tiled=True
    ).astype(columns.dtype)


def solution(mesh):
    placed = (P("mem", "space"), P(None, "space"), P(None, "space"), P(None, "space"))
    return jax.shard_map(
        shards, mesh=mesh, in_specs=placed, out_specs=P("mem", "space"), check_vma=False
    )
```

profile of v0, /device:TPU:16, one launch (start us, length us, event | category | flops | bytes accessed | tf_op | source)
XLA Modules:
  0.0 354.4 jit_solution(18122900170612398476)
XLA Ops:
  6.5 3.4 collective-permute-start
  11.9 4.5 %collective-permute-start.2 = (s32[4,256]{1,0:T(4,128)}, s32[4,256]{1,0:T(4,128)S(1)}, u32[]{:S(2)}, u32[]{:S(2)}) collective-permute-start(s32[4,256]{1,0:T(4,128)} %param.15), channel_id=1, source_target_pairs={{2,0},{4,2},{6,4},{8,6},{10,8},{12,10},{14,12},{16,14},{18,16},{20... | collective-permute-start | bytes 12296 | tf_op jit(solution)/shard_map/ppermute | solution.py:12
  18.9 3.1 copy.207
  22.0 3.8 %all-to-all-start = ((f32[32,2,8192]{2,0,1:T(8,128)}), f32[32,2,8192]{2,0,1:T(8,128)S(1)}, u32[]{:S(2)}, u32[]{:S(2)}) async-start(f32[32,2,8192]{2,0,1:T(8,128)} %bitcast.139), calls=%async_computation | async-start | bytes 4194304 | tf_op jit(solution)/shard_map/all_to_all | solution.py:51
  30.2 20.4 %all-to-all-done = f32[32,2,8192]{2,0,1:T(8,128)S(1)} async-done(((f32[32,2,8192]{2,0,1:T(8,128)}), f32[32,2,8192]{2,0,1:T(8,128)S(1)}, u32[]{:S(2)}, u32[]{:S(2)}) %all-to-all-start) | async-done | bytes 2097184 | tf_op jit(solution)/shard_map/all_to_all | solution.py:51
  50.6 2.7 copy.195
  53.3 2.9 gather_fusion
  56.3 2.5 collective-permute-start.4
  60.8 4.5 %collective-permute-start.6 = (f32[66,256]{1,0:T(8,128)S(1)}, f32[66,256]{1,0:T(8,128)S(1)}, u32[]{:S(2)}, u32[]{:S(2)}) collective-permute-start(f32[66,256]{1,0:T(8,128)S(1)} %pad_maximum_fusion), channel_id=1, source_target_pairs={{2,0},{4,2},{6,4},{8,6},{10,8},{12,10},{14,12},{16,14},{18,16},{20... | collective-permute-start | bytes 202760 | tf_op jit(solution)/shard_map/ppermute | solution.py:12
  65.3 3.3 collective-permute-start.7
  73.3 23.5 %all-reduce.5.cloned.1.call-done = f32[64,1280]{1,0:T(8,128)} async-done(((f32[64,1280]{1,0:T(8,128)}), f32[64,1280]{1,0:T(8,128)}) %all-reduce.5.cloned.1.call-update) | async-done | bytes 327696 | tf_op jit(solution)/shard_map/psum | solution.py:69
  100.0 20.3 %while.56 = (s32[]{:T(128)}, f32[64,8192]{1,0:T(8,128)S(1)}, s32[1,1280]{1,0:T(1,128)S(1)}, bf16[64,8192]{1,0:T(8,128)(2,1)S(1)}, bf16[64,1280]{1,0:T(8,128)(2,1...) while((s32[]{:T(128)}, f32[64,8192]{1,0:T(8,128)S(1)}, ...), condition=%wide.region_5.7_spmd.clone, body=%wide.region_4.6_spmd.clone.sunk | while | flops 347408384 | bytes 1010855 | solution.py:94
  100.1 2.5 fusion.98
  102.6 2.5 fusion.98
  105.1 2.5 fusion.98
  107.7 2.5 fusion.98
  110.2 2.5 fusion.98
  112.7 2.5 fusion.98
  115.3 2.5 fusion.98
  117.8 2.5 fusion.98
  120.3 2.7 copy.197
  123.0 3.0 gather_fusion.1
  126.2 3.4 collective-permute-start.8
  131.5 4.5 %collective-permute-start.10 = (f32[66,256]{1,0:T(8,128)S(1)}, f32[66,256]{1,0:T(8,128)S(1)}, u32[]{:S(2)}, u32[]{:S(2)}) collective-permute-start(f32[66,256]{1,0:T(8,128)S(1)} %pad_maximum_fusion.1), channel_id=1, source_target_pairs={{2,0},{4,2},{6,4},{8,6},{10,8},{12,10},{14,12},{16,14},{18,16},{20... | collective-permute-start | bytes 202760 | tf_op jit(solution)/shard_map/ppermute | solution.py:12
  139.4 2.9 collective-permute-done.11
  144.1 22.6 %all-reduce.7.cloned.1.call-done = f32[64,1280]{1,0:T(8,128)} async-done(((f32[64,1280]{1,0:T(8,128)}), f32[64,1280]{1,0:T(8,128)}) %all-reduce.7.cloned.1.call-update) | async-done | bytes 327696 | tf_op jit(solution)/shard_map/psum | solution.py:69
  169.8 20.3 %while.57 = (s32[]{:T(128)}, f32[64,8192]{1,0:T(8,128)S(1)}, s32[1,1280]{1,0:T(1,128)S(1)}, bf16[64,8192]{1,0:T(8,128)(2,1)S(1)}, bf16[64,1280]{1,0:T(8,128)(2,1...) while((s32[]{:T(128)}, f32[64,8192]{1,0:T(8,128)S(1)}, ...), condition=%wide.region_11.13_spmd.clone, body=%wide.region_10.12_spmd.clone.sunk | while | flops 347408384 | bytes 1010855 | solution.py:94
  169.9 2.5 fusion.102
  172.4 2.5 fusion.102
  175.0 2.5 fusion.102
  177.5 2.5 fusion.102
  180.0 2.5 fusion.102
  182.6 2.5 fusion.102
  185.1 2.5 fusion.102
  187.6 2.5 fusion.102
  190.2 2.7 copy.199
  192.9 3.0 gather_fusion.2
  196.1 3.4 collective-permute-start.12
  201.4 4.5 %collective-permute-start.14 = (f32[66,256]{1,0:T(8,128)S(1)}, f32[66,256]{1,0:T(8,128)S(1)}, u32[]{:S(2)}, u32[]{:S(2)}) collective-permute-start(f32[66,256]{1,0:T(8,128)S(1)} %pad_maximum_fusion.2), channel_id=1, source_target_pairs={{2,0},{4,2},{6,4},{8,6},{10,8},{12,10},{14,12},{16,14},{18,16},{20... | collective-permute-start | bytes 202760 | tf_op jit(solution)/shard_map/ppermute | solution.py:12
  209.3 2.9 collective-permute-done.15
  214.1 22.4 %all-reduce.9.cloned.1.call-done = f32[64,1280]{1,0:T(8,128)} async-done(((f32[64,1280]{1,0:T(8,128)}), f32[64,1280]{1,0:T(8,128)}) %all-reduce.9.cloned.1.call-update) | async-done | bytes 327696 | tf_op jit(solution)/shard_map/psum | solution.py:69
  239.7 20.3 %while.58 = (s32[]{:T(128)}, f32[64,8192]{1,0:T(8,128)S(1)}, s32[1,1280]{1,0:T(1,128)S(1)}, bf16[64,8192]{1,0:T(8,128)(2,1)S(1)}, bf16[64,1280]{1,0:T(8,128)(2,1...) while((s32[]{:T(128)}, f32[64,8192]{1,0:T(8,128)S(1)}, ...), condition=%wide.region_17.19_spmd.clone, body=%wide.region_16.18_spmd.clone.sunk | while | flops 347408384 | bytes 1010855 | solution.py:94
  239.7 2.5 fusion.106
  242.3 2.5 fusion.106
  244.8 2.5 fusion.106
  247.3 2.5 fusion.106
  249.9 2.5 fusion.106
  252.4 2.5 fusion.106
  254.9 2.5 fusion.106
  257.5 2.5 fusion.106
  260.0 2.7 copy.201
  262.7 3.0 gather_fusion.3
  265.9 3.4 collective-permute-start.16
  271.2 4.5 %collective-permute-start.18 = (f32[66,256]{1,0:T(8,128)S(1)}, f32[66,256]{1,0:T(8,128)S(1)}, u32[]{:S(2)}, u32[]{:S(2)}) collective-permute-start(f32[66,256]{1,0:T(8,128)S(1)} %pad_maximum_fusion.3), channel_id=1, source_target_pairs={{2,0},{4,2},{6,4},{8,6},{10,8},{12,10},{14,12},{16,14},{18,16},{20... | collective-permute-start | bytes 202760 | tf_op jit(solution)/shard_map/ppermute | solution.py:12
  278.5 3.5 collective-permute-done.19
  282.9 23.4 %all-reduce.11.cloned.1.call-done = f32[64,1280]{1,0:T(8,128)} async-done(((f32[64,1280]{1,0:T(8,128)}), f32[64,1280]{1,0:T(8,128)}) %all-reduce.11.cloned.1.call-update) | async-done | bytes 327696 | tf_op jit(solution)/shard_map/psum | solution.py:69
  309.5 20.3 %while.59 = (s32[]{:T(128)}, f32[64,8192]{1,0:T(8,128)S(1)}, s32[1,1280]{1,0:T(1,128)S(1)}, bf16[64,8192]{1,0:T(8,128)(2,1)S(1)}, bf16[64,1280]{1,0:T(8,128)(2,1...) while((s32[]{:T(128)}, f32[64,8192]{1,0:T(8,128)S(1)}, ...), condition=%wide.region_23.25_spmd.clone, body=%wide.region_22.24_spmd.clone.sunk | while | flops 347408384 | bytes 1010855 | solution.py:94
  309.6 2.5 fusion.110
  312.1 2.5 fusion.110
  314.6 2.5 fusion.110
  317.2 2.5 fusion.110
  322.2 2.5 fusion.110
  327.3 2.5 fusion.110
  329.9 16.3 %all_to_all.32 = bf16[2,32,8192]{2,1,0:T(8,128)(2,1)S(1)} all-to-all(bf16[2,32,8192]{2,1,0:T(8,128)(2,1)S(1)} %bitcast.140), channel_id=1, replica_groups=mesh['space'=16,'mem'=2] {'mem'}, dimensions={0} | all-to-all | bytes 2097152 | tf_op jit(solution)/shard_map/all_to_all | solution.py:95
  (225 shorter events, 55.0 us)
Async XLA Ops:
  6.5 23.5 %collective-permute-start = (s32[4,256]{1,0:T(4,128)}, s32[4,256]{1,0:T(4,128)S(1)}, u32[]{:S(2)}, u32[]{:S(2)}) collective-permute-start(s32[4,256]{1,0:T(4,128)} %param.15), channel_id=1, source_target_pairs={{0,4},{2,6},{4,8},{6,10},{8,12},{10,14},{12,16},{14,18},{16,20},{1... | collective-permute-start | bytes 12296 | tf_op jit(solution)/shard_map/ppermute | solution.py:12
  10.0 20.1 %collective-permute-start.1 = (s32[4,256]{1,0:T(4,128)}, s32[4,256]{1,0:T(4,128)S(1)}, u32[]{:S(2)}, u32[]{:S(2)}) collective-permute-start(s32[4,256]{1,0:T(4,128)} %param.15), channel_id=1, source_target_pairs={{0,2},{2,4},{4,6},{6,8},{8,10},{10,12},{12,14},{14,16},{16,18},{18... | collective-permute-start | bytes 12296 | tf_op jit(solution)/shard_map/ppermute | solution.py:12
  11.9 18.2 %collective-permute-start.2 = (s32[4,256]{1,0:T(4,128)}, s32[4,256]{1,0:T(4,128)S(1)}, u32[]{:S(2)}, u32[]{:S(2)}) collective-permute-start(s32[4,256]{1,0:T(4,128)} %param.15), channel_id=1, source_target_pairs={{2,0},{4,2},{6,4},{8,6},{10,8},{12,10},{14,12},{16,14},{18,16},{20... | collective-permute-start | bytes 12296 | tf_op jit(solution)/shard_map/ppermute | solution.py:12
  16.4 13.7 %collective-permute-start.3 = (s32[4,256]{1,0:T(4,128)}, s32[4,256]{1,0:T(4,128)S(1)}, u32[]{:S(2)}, u32[]{:S(2)}) collective-permute-start(s32[4,256]{1,0:T(4,128)} %param.15), channel_id=1, source_target_pairs={{4,0},{6,2},{8,4},{10,6},{12,8},{14,10},{16,12},{18,14},{20,16},{2... | collective-permute-start | bytes 12296 | tf_op jit(solution)/shard_map/ppermute | solution.py:12
  18.9 6.9 %copy-start = (s32[4,256]{1,0:T(4,128)S(1)}, s32[4,256]{1,0:T(4,128)}, u32[]{:S(2)}) copy-start(s32[4,256]{1,0:T(4,128)} %param.15) | copy-start | bytes 12292
  18.9 9.4 %copy-start.7 = (f32[4,256]{1,0:T(4,128)S(1)}, f32[4,256]{1,0:T(4,128)}, u32[]{:S(2)}) copy-start(f32[4,256]{1,0:T(4,128)} %param.16) | copy-start | bytes 12292
  18.9 9.4 %copy-start.8 = (f32[4,256]{1,0:T(4,128)S(1)}, f32[4,256]{1,0:T(4,128)}, u32[]{:S(2)}) copy-start(f32[4,256]{1,0:T(4,128)} %param.17) | copy-start | bytes 12292
  22.0 28.6 %all-to-all-start = ((f32[32,2,8192]{2,0,1:T(8,128)}), f32[32,2,8192]{2,0,1:T(8,128)S(1)}, u32[]{:S(2)}, u32[]{:S(2)}) async-start(f32[32,2,8192]{2,0,1:T(8,128)} %bitcast.139), calls=%async_computation | async-start | bytes 4194304 | tf_op jit(solution)/shard_map/all_to_all | solution.py:51
  25.7 71.1 %all-reduce.5.cloned.1.call-start = ((), (), s32[]{:S(2)}) async-start(), calls=%async_computation.2 | async-start | bytes 655360 | tf_op jit(solution)/shard_map/psum | solution.py:69
  56.3 13.1 %collective-permute-start.4 = (f32[66,256]{1,0:T(8,128)S(1)}, f32[66,256]{1,0:T(8,128)S(1)}, u32[]{:S(2)}, u32[]{:S(2)}) collective-permute-start(f32[66,256]{1,0:T(8,128)S(1)} %pad_maximum_fusion), channel_id=1, source_target_pairs={{0,4},{2,6},{4,8},{6,10},{8,12},{10,14},{12,16},{14,18},{16,20},{1... | collective-permute-start | bytes 202760 | tf_op jit(solution)/shard_map/ppermute | solution.py:12
  58.9 10.6 %collective-permute-start.5 = (f32[66,256]{1,0:T(8,128)S(1)}, f32[66,256]{1,0:T(8,128)S(1)}, u32[]{:S(2)}, u32[]{:S(2)}) collective-permute-start(f32[66,256]{1,0:T(8,128)S(1)} %pad_maximum_fusion), channel_id=1, source_target_pairs={{0,2},{2,4},{4,6},{6,8},{8,10},{10,12},{12,14},{14,16},{16,18},{18... | collective-permute-start | bytes 202760 | tf_op jit(solution)/shard_map/ppermute | solution.py:12
  60.8 8.7 %collective-permute-start.6 = (f32[66,256]{1,0:T(8,128)S(1)}, f32[66,256]{1,0:T(8,128)S(1)}, u32[]{:S(2)}, u32[]{:S(2)}) collective-permute-start(f32[66,256]{1,0:T(8,128)S(1)} %pad_maximum_fusion), channel_id=1, source_target_pairs={{2,0},{4,2},{6,4},{8,6},{10,8},{12,10},{14,12},{16,14},{18,16},{20... | collective-permute-start | bytes 202760 | tf_op jit(solution)/shard_map/ppermute | solution.py:12
  65.3 6.2 %collective-permute-start.7 = (f32[66,256]{1,0:T(8,128)S(1)}, f32[66,256]{1,0:T(8,128)S(1)}, u32[]{:S(2)}, u32[]{:S(2)}) collective-permute-start(f32[66,256]{1,0:T(8,128)S(1)} %pad_maximum_fusion), channel_id=1, source_target_pairs={{4,0},{6,2},{8,4},{10,6},{12,8},{14,10},{16,12},{18,14},{20,16},{2... | collective-permute-start | bytes 202760 | tf_op jit(solution)/shard_map/ppermute | solution.py:12
  72.4 94.3 %all-reduce.7.cloned.1.call-start = ((), (), s32[]{:S(2)}) async-start(), calls=%async_computation.3 | async-start | bytes 655360 | tf_op jit(solution)/shard_map/psum | solution.py:69
  120.3 5.9 %copy-start.11 = (pred[256]{0:T(512)(128)(4,1)S(1)}, pred[256]{0:T(512)(128)(4,1)}, u32[]{:S(2)}) copy-start(pred[256]{0:T(512)(128)(4,1)} %get-tuple-element.724) | copy-start | bytes 772
  120.3 5.9 %copy-start.14 = (pred[256]{0:T(512)(128)(4,1)S(1)}, pred[256]{0:T(512)(128)(4,1)}, u32[]{:S(2)}) copy-start(pred[256]{0:T(512)(128)(4,1)} %compare_and_fusion.2) | copy-start | bytes 772
  120.3 5.9 %copy-start.5 = (f32[1,256]{1,0:T(1,128)S(1)}, f32[1,256]{1,0:T(1,128)}, u32[]{:S(2)}) copy-start(f32[1,256]{1,0:T(1,128)} %get-tuple-element.807) | copy-start | bytes 3076
  120.3 5.9 %copy-start.6 = (f32[1,256]{1,0:T(1,128)S(1)}, f32[1,256]{1,0:T(1,128)}, u32[]{:S(2)}) copy-start(f32[1,256]{1,0:T(1,128)} %get-tuple-element.818) | copy-start | bytes 3076
  126.2 13.1 %collective-permute-start.8 = (f32[66,256]{1,0:T(8,128)S(1)}, f32[66,256]{1,0:T(8,128)S(1)}, u32[]{:S(2)}, u32[]{:S(2)}) collective-permute-start(f32[66,256]{1,0:T(8,128)S(1)} %pad_maximum_fusion.1), channel_id=1, source_target_pairs={{0,4},{2,6},{4,8},{6,10},{8,12},{10,14},{12,16},{14,18},{16,20},{1... | collective-permute-start | bytes 202760 | tf_op jit(solution)/shard_map/ppermute | solution.py:12
  129.6 9.7 %collective-permute-start.9 = (f32[66,256]{1,0:T(8,128)S(1)}, f32[66,256]{1,0:T(8,128)S(1)}, u32[]{:S(2)}, u32[]{:S(2)}) collective-permute-start(f32[66,256]{1,0:T(8,128)S(1)} %pad_maximum_fusion.1), channel_id=1, source_target_pairs={{0,2},{2,4},{4,6},{6,8},{8,10},{10,12},{12,14},{14,16},{16,18},{18... | collective-permute-start | bytes 202760 | tf_op jit(solution)/shard_map/ppermute | solution.py:12
  131.5 7.8 %collective-permute-start.10 = (f32[66,256]{1,0:T(8,128)S(1)}, f32[66,256]{1,0:T(8,128)S(1)}, u32[]{:S(2)}, u32[]{:S(2)}) collective-permute-start(f32[66,256]{1,0:T(8,128)S(1)} %pad_maximum_fusion.1), channel_id=1, source_target_pairs={{2,0},{4,2},{6,4},{8,6},{10,8},{12,10},{14,12},{16,14},{18,16},{20... | collective-permute-start | bytes 202760 | tf_op jit(solution)/shard_map/ppermute | solution.py:12
  136.1 6.2 %collective-permute-start.11 = (f32[66,256]{1,0:T(8,128)S(1)}, f32[66,256]{1,0:T(8,128)S(1)}, u32[]{:S(2)}, u32[]{:S(2)}) collective-permute-start(f32[66,256]{1,0:T(8,128)S(1)} %pad_maximum_fusion.1), channel_id=1, source_target_pairs={{4,0},{6,2},{8,4},{10,6},{12,8},{14,10},{16,12},{18,14},{20,16},{2... | collective-permute-start | bytes 202760 | tf_op jit(solution)/shard_map/ppermute | solution.py:12
  143.1 93.4 %all-reduce.9.cloned.1.call-start = ((), (), s32[]{:S(2)}) async-start(), calls=%async_computation.4 | async-start | bytes 655360 | tf_op jit(solution)/shard_map/psum | solution.py:69
  190.1 5.9 %copy-start.10 = (pred[256]{0:T(512)(128)(4,1)S(1)}, pred[256]{0:T(512)(128)(4,1)}, u32[]{:S(2)}) copy-start(pred[256]{0:T(512)(128)(4,1)} %get-tuple-element.723) | copy-start | bytes 772
  190.1 5.9 %copy-start.13 = (pred[256]{0:T(512)(128)(4,1)S(1)}, pred[256]{0:T(512)(128)(4,1)}, u32[]{:S(2)}) copy-start(pred[256]{0:T(512)(128)(4,1)} %compare_and_fusion.1) | copy-start | bytes 772
  190.1 5.9 %copy-start.3 = (f32[1,256]{1,0:T(1,128)S(1)}, f32[1,256]{1,0:T(1,128)}, u32[]{:S(2)}) copy-start(f32[1,256]{1,0:T(1,128)} %get-tuple-element.809) | copy-start | bytes 3076
  190.2 5.9 %copy-start.4 = (f32[1,256]{1,0:T(1,128)S(1)}, f32[1,256]{1,0:T(1,128)}, u32[]{:S(2)}) copy-start(f32[1,256]{1,0:T(1,128)} %get-tuple-element.816) | copy-start | bytes 3076
  196.1 13.1 %collective-permute-start.12 = (f32[66,256]{1,0:T(8,128)S(1)}, f32[66,256]{1,0:T(8,128)S(1)}, u32[]{:S(2)}, u32[]{:S(2)}) collective-permute-start(f32[66,256]{1,0:T(8,128)S(1)} %pad_maximum_fusion.2), channel_id=1, source_target_pairs={{0,4},{2,6},{4,8},{6,10},{8,12},{10,14},{12,16},{14,18},{16,20},{1... | collective-permute-start | bytes 202760 | tf_op jit(solution)/shard_map/ppermute | solution.py:12
  199.5 9.7 %collective-permute-start.13 = (f32[66,256]{1,0:T(8,128)S(1)}, f32[66,256]{1,0:T(8,128)S(1)}, u32[]{:S(2)}, u32[]{:S(2)}) collective-permute-start(f32[66,256]{1,0:T(8,128)S(1)} %pad_maximum_fusion.2), channel_id=1, source_target_pairs={{0,2},{2,4},{4,6},{6,8},{8,10},{10,12},{12,14},{14,16},{16,18},{18... | collective-permute-start | bytes 202760 | tf_op jit(solution)/shard_map/ppermute | solution.py:12
  201.4 7.8 %collective-permute-start.14 = (f32[66,256]{1,0:T(8,128)S(1)}, f32[66,256]{1,0:T(8,128)S(1)}, u32[]{:S(2)}, u32[]{:S(2)}) collective-permute-start(f32[66,256]{1,0:T(8,128)S(1)} %pad_maximum_fusion.2), channel_id=1, source_target_pairs={{2,0},{4,2},{6,4},{8,6},{10,8},{12,10},{14,12},{16,14},{18,16},{20... | collective-permute-start | bytes 202760 | tf_op jit(solution)/shard_map/ppermute | solution.py:12
  206.0 6.2 %collective-permute-start.15 = (f32[66,256]{1,0:T(8,128)S(1)}, f32[66,256]{1,0:T(8,128)S(1)}, u32[]{:S(2)}, u32[]{:S(2)}) collective-permute-start(f32[66,256]{1,0:T(8,128)S(1)} %pad_maximum_fusion.2), channel_id=1, source_target_pairs={{4,0},{6,2},{8,4},{10,6},{12,8},{14,10},{16,12},{18,14},{20,16},{2... | collective-permute-start | bytes 202760 | tf_op jit(solution)/shard_map/ppermute | solution.py:12
  213.0 93.4 %all-reduce.11.cloned.1.call-start = ((), (), s32[]{:S(2)}) async-start(), calls=%async_computation.5 | async-start | bytes 655360 | tf_op jit(solution)/shard_map/psum | solution.py:69
  260.0 5.9 %copy-start.9 = (pred[256]{0:T(512)(128)(4,1)S(1)}, pred[256]{0:T(512)(128)(4,1)}, u32[]{:S(2)}) copy-start(pred[256]{0:T(512)(128)(4,1)} %get-tuple-element.722) | copy-start | bytes 772
  260.0 5.9 %copy-start.12 = (pred[256]{0:T(512)(128)(4,1)S(1)}, pred[256]{0:T(512)(128)(4,1)}, u32[]{:S(2)}) copy-start(pred[256]{0:T(512)(128)(4,1)} %compare_and_fusion) | copy-start | bytes 772
  260.0 5.9 %copy-start.1 = (f32[1,256]{1,0:T(1,128)S(1)}, f32[1,256]{1,0:T(1,128)}, u32[]{:S(2)}) copy-start(f32[1,256]{1,0:T(1,128)} %get-tuple-element.806) | copy-start | bytes 3076
  260.0 5.9 %copy-start.2 = (f32[1,256]{1,0:T(1,128)S(1)}, f32[1,256]{1,0:T(1,128)}, u32[]{:S(2)}) copy-start(f32[1,256]{1,0:T(1,128)} %get-tuple-element.819) | copy-start | bytes 3076
  265.9 12.5 %collective-permute-start.16 = (f32[66,256]{1,0:T(8,128)S(1)}, f32[66,256]{1,0:T(8,128)S(1)}, u32[]{:S(2)}, u32[]{:S(2)}) collective-permute-start(f32[66,256]{1,0:T(8,128)S(1)} %pad_maximum_fusion.3), channel_id=1, source_target_pairs={{0,4},{2,6},{4,8},{6,10},{8,12},{10,14},{12,16},{14,18},{16,20},{1... | collective-permute-start | bytes 202760 | tf_op jit(solution)/shard_map/ppermute | solution.py:12
  269.3 9.1 %collective-permute-start.17 = (f32[66,256]{1,0:T(8,128)S(1)}, f32[66,256]{1,0:T(8,128)S(1)}, u32[]{:S(2)}, u32[]{:S(2)}) collective-permute-start(f32[66,256]{1,0:T(8,128)S(1)} %pad_maximum_fusion.3), channel_id=1, source_target_pairs={{0,2},{2,4},{4,6},{6,8},{8,10},{10,12},{12,14},{14,16},{16,18},{18... | collective-permute-start | bytes 202760 | tf_op jit(solution)/shard_map/ppermute | solution.py:12
  271.2 7.3 %collective-permute-start.18 = (f32[66,256]{1,0:T(8,128)S(1)}, f32[66,256]{1,0:T(8,128)S(1)}, u32[]{:S(2)}, u32[]{:S(2)}) collective-permute-start(f32[66,256]{1,0:T(8,128)S(1)} %pad_maximum_fusion.3), channel_id=1, source_target_pairs={{2,0},{4,2},{6,4},{8,6},{10,8},{12,10},{14,12},{16,14},{18,16},{20... | collective-permute-start | bytes 202760 | tf_op jit(solution)/shard_map/ppermute | solution.py:12
  275.8 6.2 %collective-permute-start.19 = (f32[66,256]{1,0:T(8,128)S(1)}, f32[66,256]{1,0:T(8,128)S(1)}, u32[]{:S(2)}, u32[]{:S(2)}) collective-permute-start(f32[66,256]{1,0:T(8,128)S(1)} %pad_maximum_fusion.3), channel_id=1, source_target_pairs={{4,0},{6,2},{8,4},{10,6},{12,8},{14,10},{16,12},{18,14},{20,16},{2... | collective-permute-start | bytes 202760 | tf_op jit(solution)/shard_map/ppermute | solution.py:12
Sparse Core Ops, SparseCore 0:
  72.5 24.2 all-reduce.4
  143.2 23.3 all-reduce.6
  213.1 23.3 all-reduce.8
  282.9 23.3 all-reduce.10
where the time goes:
time: 358 us; the launch traced here: 354 us
  waiting for transfers between devices  124 us (35%)
  matrix products  79.2 us (22%)
  starting transfers between devices  65.6 us (18%)
  local copies, waits for them, and re-layouts  31.5 us (9%)
  other arithmetic  22.6 us (6%)
  blocking collectives  16.3 us (5%)
  between operations  14.1 us (4%)
    psum x4, waiting for transfers between devices, shards(): band_prior = lax.psum(band_prior, 'mem')  92 us
    dot_general x32, matrix products, update(): increment = jnp.dot(band_weight, gain, preferred_element_type=jnp.float32)  79.2 us
    ppermute x20, starting transfers between devices, shifted(): return lax.ppermute(block, axis, route)  61.5 us
    all_to_all x1, waiting for transfers between devices, shards(): lax.all_to_all(state, 'mem', split_axis=1, concat_axis=0, tiled=True)  20.4 us
    all_to_all x1, blocking collectives, shards(): lax.all_to_all(columns.astype(jnp.bfloat16), 'mem', split_axis=0, concat_...  16.3 us
    gather x8, local copies, waits for them, and re-layouts, shards(): picked = jnp.take(columns, jnp.clip(local_col, 0, width - 1), axis=1)  12.4 us
    ppermute x20, waiting for transfers between devices, shifted(): return lax.ppermute(block, axis, route)  11.5 us
    while x3, local copies, waits for them, and re-layouts, shards(): columns = lax.fori_loop(0, block_count, update, columns)  8.09 us
  transfers between devices with their start and end apart: 25, of which 9 were waited for; matrix products, arithmetic and copies ran while one was open for 4% of the time, Pallas kernels for 0%

commit v1 on v0

v1 whole, which is shorter than its diff:
```python
import functools

import jax
import jax.numpy as jnp
from jax import lax
from jax.experimental import pallas as pl
from jax.experimental.pallas import tpu as pltpu
from jax.sharding import PartitionSpec as P

RADIUS = 32768
OFFSETS = (-2, 2, -1, 1)
SLOT = {-2: 0, 0: 1, 2: 2, -1: 3, 1: 4}
CHUNK = 256
f32, bf16 = jnp.float32, jnp.bfloat16


def gather_kernel(idx_ref, state_ref, out_ref):
    half_members, cols = state_ref.shape
    batches, obs_dev = idx_ref.shape
    base = lax.axis_index("space") * cols
    lanes = lax.broadcasted_iota(jnp.int32, (half_members, 128), 1)
    for batch in range(batches):
        for part in range(obs_dev // 128):
            def pick(step, acc):
                for inner in range(8):
                    t = step * 8 + inner
                    col = idx_ref[batch, part * 128 + t] - base
                    hi = lax.shift_right_logical(col, 7)
                    lo = col & 127
                    tile = state_ref[:, pl.ds(pl.multiple_of(hi * 128, 128), 128)]
                    moved = pltpu.roll(tile, (t - lo) & 127, 1)
                    acc = jnp.where(lanes == t, moved, acc)
                return acc
            at = batch * obs_dev + part * 128
            out_ref[:, at:at + 128] = lax.fori_loop(
                0, 16, pick, jnp.zeros((half_members, 128), f32))


def kernel(
    n_space, batches, obs_dev, half_members, cols,
    g_send, state_ref, pos_ref, value_ref, var_ref, out_ref,
    g_recv, g_ref, x_send, x_recv, cur, e_send, e_recv,
    pos_own, pos_nb, aw, a_t, coef, moment,
    g_sems, x_sems, e_sems, pos_ssem, pos_rsem, aw_ssem, aw_rsem,
):
    space = lax.axis_index("space")
    mem = lax.axis_index("mem")
    other = 1 - mem
    width = cols // 2
    members = 2 * half_members
    own_start = mem * width
    other_start = other * width
    base = space * cols
    block = cols / RADIUS
    partner = {"mem": other}
    valid = {o: (space + o >= 0) & (space + o < n_space) for o in OFFSETS}

    barrier = pltpu.get_barrier_semaphore()
    pl.semaphore_signal(barrier, inc=1, device_id=partner, device_id_type=pl.DeviceIdType.MESH)
    for o in OFFSETS:
        @pl.when(valid[o])
        def _(o=o):
            pl.semaphore_signal(
                barrier, inc=1, device_id={"space": space + o},
                device_id_type=pl.DeviceIdType.MESH)

    def g_copy(part):
        span = pl.ds(0, obs_dev) if part == 0 else pl.ds(obs_dev, (batches - 1) * obs_dev)
        return pltpu.make_async_remote_copy(
            src_ref=g_send.at[:, span], dst_ref=g_recv.at[:, span],
            send_sem=g_sems.at[0, part], recv_sem=g_sems.at[1, part],
            device_id=partner, device_id_type=pl.DeviceIdType.MESH)

    x_copy = pltpu.make_async_remote_copy(
        src_ref=x_send, dst_ref=x_recv, send_sem=x_sems.at[0], recv_sem=x_sems.at[1],
        device_id=partner, device_id_type=pl.DeviceIdType.MESH)

    groups = 8
    group_width = width // groups

    def e_copy(group):
        span = pl.ds(pl.multiple_of(group * group_width, 128), group_width)
        return pltpu.make_async_remote_copy(
            src_ref=e_send.at[:, span], dst_ref=e_recv.at[:, span],
            send_sem=e_sems.at[0, group], recv_sem=e_sems.at[1, group],
            device_id=partner, device_id_type=pl.DeviceIdType.MESH)

    def pos_copy(o):
        i = OFFSETS.index(o)
        back = OFFSETS.index(-o)
        return pltpu.make_async_remote_copy(
            src_ref=pos_own, dst_ref=pos_nb.at[back],
            send_sem=pos_ssem.at[i], recv_sem=pos_rsem.at[back],
            device_id={"space": space + o}, device_id_type=pl.DeviceIdType.MESH)

    def pos_wait(o):
        i = OFFSETS.index(o)
        pltpu.make_async_remote_copy(
            src_ref=pos_own, dst_ref=pos_nb.at[i],
            send_sem=pos_ssem.at[i], recv_sem=pos_rsem.at[i],
            device_id={"space": space + o}, device_id_type=pl.DeviceIdType.MESH).wait_recv()

    def aw_copy(batch, o):
        i = OFFSETS.index(o)
        back = OFFSETS.index(-o)
        return pltpu.make_async_remote_copy(
            src_ref=aw.at[batch, SLOT[0]], dst_ref=aw.at[batch, SLOT[-o]],
            send_sem=aw_ssem.at[batch, i], recv_sem=aw_rsem.at[batch, back],
            device_id={"space": space + o}, device_id_type=pl.DeviceIdType.MESH)

    def aw_wait(batch, o):
        i = OFFSETS.index(o)
        pltpu.make_async_remote_copy(
            src_ref=aw.at[batch, SLOT[0]], dst_ref=aw.at[batch, SLOT[o]],
            send_sem=aw_ssem.at[batch, i], recv_sem=aw_rsem.at[batch, i],
            device_id={"space": space + o}, device_id_type=pl.DeviceIdType.MESH).wait_recv()

    pos_own[...] = jnp.zeros_like(pos_own)
    pos_own[:batches, :] = (pos_ref[...] - base - cols // 2).astype(f32) * (1.0 / RADIUS)
    for o in OFFSETS:
        @pl.when(jnp.logical_not(valid[o]))
        def _(o=o):
            pos_nb[OFFSETS.index(o)] = jnp.zeros(pos_nb.shape[1:], f32)
            for batch in range(batches):
                aw[batch, SLOT[o]] = jnp.zeros(aw.shape[2:], bf16)

    count = 1
    for o in OFFSETS:
        count = count + jnp.where(valid[o], 1, 0)
    pl.semaphore_wait(barrier, count)
    g_copy(0).start()
    for o in OFFSETS:
        @pl.when(valid[o])
        def _(o=o):
            pos_copy(o).start()

    def cast(i, carry):
        at = pl.multiple_of(i * 1024, 128)
        x_send[:, pl.ds(at, 1024)] = state_ref[
            :, pl.ds(pl.multiple_of(other_start + at, 128), 1024)].astype(bf16)
        cur[:half_members, pl.ds(at, 1024)] = state_ref[
            :, pl.ds(pl.multiple_of(own_start + at, 128), 1024)]
        return carry
    lax.fori_loop(0, width // 1024, cast, 0)
    x_copy.start()
    g_copy(1).start()
    g_ref[:half_members, :] = g_send[...]

    def increment(batch, now, u):
        mean = jnp.sum(now, axis=0, keepdims=True) * (1.0 / members)
        anomaly = now - mean
        spread = anomaly.astype(bf16)
        total = jnp.dot(
            moment[:, :3 * members],
            jnp.concatenate(
                [spread, (anomaly * u).astype(bf16), (anomaly * (u * u)).astype(bf16)], axis=0),
            preferred_element_type=f32)
        for slot in range(3):
            cov = jnp.dot(
                a_t[slot * obs_dev:(slot + 1) * obs_dev, :], spread, preferred_element_type=f32)
            c = coef[slot]
            if slot == 0:
                t = jnp.maximum(c - u, 0.0)
            elif slot == 1:
                t = jnp.maximum(1.0 - jnp.abs(c - u), 0.0)
            else:
                t = jnp.maximum(c + u, 0.0)
            gain = (t * t * cov).astype(bf16)
            total = total + jnp.dot(
                aw[batch, slot, members:2 * members, :], gain, preferred_element_type=f32)
        return total

    def build(batch):
        def row(o):
            if o == 0:
                return pos_own[batch:batch + 1, :]
            return pos_nb[OFFSETS.index(o), batch:batch + 1, :] + o * block
        for o in (-2, 0, 2):
            slot = SLOT[o]
            q = row(o)
            c = q if o == 0 else (1.0 + q if o < 0 else 1.0 - q)
            coef[slot] = jnp.transpose(jnp.broadcast_to(c, (CHUNK, obs_dev)))
            a_t[slot * obs_dev:(slot + 1) * obs_dev, :] = jnp.transpose(
                aw[batch, slot, :members, :].astype(f32)).astype(bf16)
        sums = 0.0
        for o in (-1, 1):
            slot = SLOT[o]
            q = row(o)
            c = 1.0 + q if o < 0 else 1.0 - q
            a = aw[batch, slot, :members, :].astype(f32)
            rhs = jnp.concatenate([a * (c * c), a * (2.0 * o * c), a], axis=0).astype(bf16)
            sums = sums + lax.dot_general(
                aw[batch, slot, members:2 * members, :], rhs, (((1,), (1,)), ((), ())),
                preferred_element_type=f32)
        moment[:, :3 * members] = sums.astype(bf16)

    lane_u = lax.broadcasted_iota(jnp.int32, (1, CHUNK), 1)

    def chunk_update(batch, at):
        now = cur[:, pl.ds(at, CHUNK)]
        u = (lane_u + (own_start + at - cols // 2)).astype(f32) * (1.0 / RADIUS)
        return now + increment(batch, now, u)

    def full_update(batch):
        def step(i, carry):
            at = pl.multiple_of(i * CHUNK, CHUNK)
            cur[:, pl.ds(at, CHUNK)] = chunk_update(batch, at)
            return carry
        lax.fori_loop(0, width // CHUNK, step, 0)

    def last_update(batch):
        per = group_width // CHUNK

        def group_step(group, carry):
            def step(i, inner):
                at = pl.multiple_of((group * per + i) * CHUNK, CHUNK)
                done = chunk_update(batch, at)
                out_ref[:, pl.ds(pl.multiple_of(own_start + at, CHUNK), CHUNK)] = done[:half_members]
                e_send[:, pl.ds(at, CHUNK)] = (
                    done[half_members:] - x_recv[:, pl.ds(at, CHUNK)].astype(f32)).astype(bf16)
                return inner
            lax.fori_loop(0, per, step, 0)
            e_copy(group).start()
            return carry
        lax.fori_loop(0, groups, group_step, 0)

    def summarize(batch):
        span = slice(batch * obs_dev, (batch + 1) * obs_dev)
        prior = g_ref[:, span]
        values = value_ref[batch:batch + 1, :]
        variances = var_ref[batch:batch + 1, :]
        obs_mean = jnp.sum(prior, axis=0, keepdims=True) * (1.0 / members)
        anomaly = prior - obs_mean
        spread = jnp.sum(anomaly * anomaly, axis=0, keepdims=True) * (1.0 / (members - 1)) + 1e-06
        post_var = 1.0 / (1.0 / spread + 1.0 / variances)
        post_mean = post_var * (obs_mean / spread + values / variances)
        change = post_mean - obs_mean + (jnp.sqrt(post_var / spread) - 1.0) * anomaly
        aw[batch, SLOT[0], :members, :] = anomaly.astype(bf16)
        aw[batch, SLOT[0], members:, :] = (change / ((members - 1) * spread)).astype(bf16)

    for batch in range(batches):
        if batch == 0:
            g_copy(0).wait_recv()
            g_ref[half_members:, :obs_dev] = g_recv[:, :obs_dev]
        summarize(batch)
        for o in OFFSETS:
            @pl.when(valid[o])
            def _(o=o):
                aw_copy(batch, o).start()
        if batch == 0:
            g_copy(1).wait_recv()
            g_ref[half_members:, obs_dev:] = g_recv[:, obs_dev:]
            for o in OFFSETS:
                @pl.when(valid[o])
                def _(o=o):
                    pos_wait(o)
        else:
            if batch == 1:
                x_copy.wait_recv()

                def widen(i, carry):
                    at = pl.multiple_of(i * 1024, 128)
                    cur[half_members:, pl.ds(at, 1024)] = x_recv[:, pl.ds(at, 1024)].astype(f32)
                    return carry
                lax.fori_loop(0, width // 1024, widen, 0)
            full_update(batch - 1)
        for o in OFFSETS:
            @pl.when(valid[o])
            def _(o=o):
                aw_wait(batch, o)
        build(batch)
        for later in range(batch + 1, batches):
            span = slice(later * obs_dev, (later + 1) * obs_dev)
            now = g_ref[:, span]
            g_ref[:, span] = now + increment(batch, now, pos_own[later:later + 1, :])
    last_update(batches - 1)

    def finish(group, carry):
        e_copy(group).wait_recv()
        at = pl.multiple_of(group * group_width, 128)
        there = pl.ds(pl.multiple_of(other_start + at, 128), group_width)
        out_ref[:, there] = state_ref[:, there] + e_recv[:, pl.ds(at, group_width)].astype(f32)
        return carry
    lax.fori_loop(0, groups, finish, 0)

    g_copy(0).wait_send()
    g_copy(1).wait_send()
    x_copy.wait_send()
    lax.fori_loop(0, groups, lambda g, c: (e_copy(g).wait_send(), c)[1], 0)
    for o in OFFSETS:
        @pl.when(valid[o])
        def _(o=o):
            pos_copy(o).wait_send()
            for batch in range(batches):
                aw_copy(batch, o).wait_send()


def shards(n_space, state, obs_index, obs_value, obs_var):
    half_members, cols = state.shape
    batches, obs_dev = obs_index.shape
    members, width = 2 * half_members, cols // 2
    vmem = pl.BlockSpec(memory_space=pltpu.VMEM)
    smem = pl.BlockSpec(memory_space=pltpu.SMEM)
    n_obs = batches * obs_dev
    dma = pltpu.SemaphoreType.DMA
    flops = 4 * batches * members * (3 * obs_dev + 192) * width
    gathered = pl.pallas_call(
        gather_kernel,
        out_shape=jax.ShapeDtypeStruct((half_members, n_obs), f32),
        in_specs=[smem, vmem],
        out_specs=vmem,
        compiler_params=pltpu.CompilerParams(vmem_limit_bytes=32 * 1024 * 1024),
    )(obs_index, state)
    return pl.pallas_call(
        functools.partial(kernel, n_space, batches, obs_dev, half_members, cols),
        out_shape=jax.ShapeDtypeStruct(state.shape, f32),
        in_specs=[vmem, vmem, vmem, vmem, vmem],
        out_specs=vmem,
        scratch_shapes=[
            pltpu.VMEM((half_members, n_obs), f32),
            pltpu.VMEM((members, n_obs), f32),
            pltpu.VMEM((half_members, width), bf16),
            pltpu.VMEM((half_members, width), bf16),
            pltpu.VMEM((members, width), f32),
            pltpu.VMEM((half_members, width), bf16),
            pltpu.VMEM((half_members, width), bf16),
            pltpu.VMEM((8, obs_dev), f32),
            pltpu.VMEM((4, 8, obs_dev), f32),
            pltpu.VMEM((batches, 5, 2 * members, obs_dev), bf16),
            pltpu.VMEM((3 * obs_dev, members), bf16),
            pltpu.VMEM((3, obs_dev, CHUNK), f32),
            pltpu.VMEM((members, 256), bf16),
            dma((2, 2)), dma((2,)), dma((2, 8)), dma((4,)), dma((4,)),
            dma((batches, 4)), dma((batches, 4)),
        ],
        compiler_params=pltpu.CompilerParams(
            collective_id=0, has_side_effects=True, vmem_limit_bytes=48 * 1024 * 1024),
        cost_estimate=pl.CostEstimate(
            flops=flops, bytes_accessed=2 * state.size * 4, transcendentals=n_obs),
    )(gathered, state, obs_index, obs_value, obs_var)


def solution(mesh):
    placed = (P("mem", "space"), P(None, "space"), P(None, "space"), P(None, "space"))
    return jax.shard_map(
        functools.partial(shards, mesh.shape["space"]), mesh=mesh, in_specs=placed,
        out_specs=P("mem", "space"), check_vma=False)
```

time: 358 us -> 140 us (0.39)
  Pallas kernels: 0 us -> 135 us
  waiting for transfers between devices: 124 us -> 0 us
  matrix products: 79.2 us -> 0 us
  starting transfers between devices: 65.6 us -> 0 us
  local copies, waits for them, and re-layouts: 31.5 us -> 3.61 us
  other arithmetic: 22.6 us -> 0 us
  blocking collectives: 16.3 us -> 0 us
  between operations: 14.1 us -> 0.05 us
    pallas_call x0 -> x2, Pallas kernels: none -> 135 us  [the longest x1 121 us: shards(): pl.pallas_call(functools.partial(kernel, n_space, batches, obs_dev, half_...]
    psum x4 -> x0, waiting for transfers between devices: 92 us -> none  [shards(): band_prior = lax.psum(band_prior, 'mem')]
    dot_general x32 -> x0, matrix products: 79.2 us -> none  [update(): increment = jnp.dot(band_weight, gain, preferred_element_type=jnp.float32)]
    ppermute x20 -> x0, starting transfers between devices: 61.5 us -> none  [shifted(): return lax.ppermute(block, axis, route)]
    all_to_all x1 -> x0, waiting for transfers between devices: 20.4 us -> none  [shards(): lax.all_to_all(state, 'mem', split_axis=1, concat_axis=0, tiled=True)]
    all_to_all x1 -> x0, blocking collectives: 16.3 us -> none  [shards(): lax.all_to_all(columns.astype(jnp.bfloat16), 'mem', split_axis=0, concat_...]
    gather x8 -> x0, local copies, waits for them, and re-layouts: 12.4 us -> none  [shards(): picked = jnp.take(columns, jnp.clip(local_col, 0, width - 1), axis=1)]
    ppermute x20 -> x0, waiting for transfers between devices: 11.5 us -> none  [shifted(): return lax.ppermute(block, axis, route)]
  transfers between devices with their start and end apart: 25 -> 0, of which waited for: 9 -> 0; matrix products, arithmetic and copies ran while one was open for 4% -> 0% of each run, Pallas kernels for 0% -> 0%
where the time goes in v1:
time: 140 us; the launch traced here: 138 us
  Pallas kernels  135 us (96%)
  local copies, waits for them, and re-layouts  3.61 us (3%)
    pallas_call x1, Pallas kernels, shards(): pl.pallas_call(functools.partial(kernel, n_space, batches, obs_dev, half_...  121 us
    pallas_call x1, Pallas kernels, shards(): pl.pallas_call(gather_kernel, out_shape=jax.ShapeDtypeStruct((half_member...  14 us
    unnamed x13, local copies, waits for them, and re-layouts  3.61 us

profile of v1, /device:TPU:16, one launch (start us, length us, event | category | flops | bytes accessed | tf_op | source)
XLA Modules:
  0.0 138.2 jit_solution(4233802012065729117)
XLA Ops:
  0.0 0.0 copy-start
  0.0 1.6 %copy-done = f32[32,16384]{1,0:T(8,128)S(1)} copy-done((f32[32,16384]{1,0:T(8,128)S(1)}, f32[32,16384]{1,0:T(8,128)}, u32[]{:S(2)}) %copy-start) | copy-done | bytes 2097176
  1.6 0.0 copy-start.2
  1.6 0.7 copy-done.2
  2.3 0.0 copy-start.1
  2.3 0.0 copy-start.3
  2.3 0.0 copy-start.4
  2.3 0.0 copy-start.5
  2.3 14.0 %shard_map.46.g_send = f32[32,1024]{1,0:T(8,128)S(1)} custom-call(s32[4,256]{1,0:T(4,128)S(1)} %copy-done.2, f32[32,16384]{1,0:T(8,128)S(1)} %copy-done), custom_call_target="tpu_custom_call" | custom-call | tf_op jit(solution)/shard_map/pallas_call | solution.py:307
  16.3 0.0 copy-done.1
  16.3 0.0 copy-done.3
  16.3 0.0 copy-done.4
  16.4 0.0 copy-done.5
  16.4 120.5 %shard_map.47 = f32[32,16384]{1,0:T(8,128)S(1)} custom-call(f32[32,1024]{1,0:T(8,128)S(1)} %shard_map.46.g_send, f32[32,16384]{1,0:T(8,128)S(1)} %copy-done.1, s32[4,256]{1,0:T(4,128)S(1)} %copy-done.3, f32[4,256]{1,0:T(4,128)S(1)} %copy-done.4, f32[4,256]{1,0:T(4,128)S(1)} %copy-done.5), custom_call_target="tpu_custom_call" | custom-call | flops 8053063680 | bytes 4194304 | tf_op jit(solution)/shard_map/pallas_call | solution.py:314
  136.9 1.3 copy.6
Async XLA Ops:
  0.0 1.6 %copy-start = (f32[32,16384]{1,0:T(8,128)S(1)}, f32[32,16384]{1,0:T(8,128)}, u32[]{:S(2)}) copy-start(f32[32,16384]{1,0:T(8,128)} %state_ref.3) | copy-start | bytes 6291460
  1.6 0.7 copy-start.2
  2.3 14.0 %copy-start.1 = (f32[32,16384]{1,0:T(8,128)S(1)}, f32[32,16384]{1,0:T(8,128)}, u32[]{:S(2)}) copy-start(f32[32,16384]{1,0:T(8,128)} %state_ref.3) | copy-start | bytes 6291460
  2.3 14.1 %copy-start.3 = (s32[4,256]{1,0:T(4,128)S(1)}, s32[4,256]{1,0:T(4,128)}, u32[]{:S(2)}) copy-start(s32[4,256]{1,0:T(4,128)} %pos_ref.1) | copy-start | bytes 12292
  2.3 14.1 %copy-start.4 = (f32[4,256]{1,0:T(4,128)S(1)}, f32[4,256]{1,0:T(4,128)}, u32[]{:S(2)}) copy-start(f32[4,256]{1,0:T(4,128)} %value_ref.1) | copy-start | bytes 12292
  2.3 14.1 %copy-start.5 = (f32[4,256]{1,0:T(4,128)S(1)}, f32[4,256]{1,0:T(4,128)}, u32[]{:S(2)}) copy-start(f32[4,256]{1,0:T(4,128)} %var_ref.1) | copy-start | bytes 12292
